TPU v7x, 512 devices: a whole 4x4x16 slice. The times are simulated.
512 devices in a mesh: leaf: 32 (over x_hi, z), grid: 16 (over x_lo, y, core).
Axes of the slice: x: 4 (x_hi: 2, x_lo: 2; x = x_hi * 2 + x_lo), y: 4, z: 16, core: 2. Of those that a mesh axis runs over, the one named last changes fastest.
Arguments:
- ancestor_inverse: bfloat16 [2048, 2048], P('grid', 'leaf')
- factor_block: bfloat16 [32, 2048, 4096], P('leaf', 'grid'), may hold values from -0.25 to 0.25
- block_pattern: int32 [32, 16], P('leaf'), may hold values 0 or 1
- pivot_inverse: float32 [32, 4096], P('leaf', 'grid'), may hold values from 0.5 to 2
Outputs:
- cross_cov: bfloat16 [32, 2048, 4096], P('leaf', 'grid')
- variances: float32 [32, 4096], P('leaf', 'grid')
All inputs are finite; a program needn't handle non-finite values. No bound on the sum of `block_pattern` on one device may be relied on, other than what follows from the above.
Results may differ from a plain program's by a relative error of at most 0.0004.
Values may be sent and summed in bfloat16 or wider, within the bound.
A program may use at most 64 MiB of HBM per device.

v0:
```python
import jax
import jax.numpy as jnp
from jax import lax
from jax.sharding import PartitionSpec as P


def on_device(ancestor_inverse, factor_block, block_pattern, pivot_inverse):
    row_count = factor_block.shape[1]
    whole_rows = ancestor_inverse.shape[1] * lax.axis_size("leaf")
    rows_per = whole_rows // block_pattern.shape[1]
    first_row = lax.axis_index("grid") * row_count
    row_ids = (first_row + jnp.arange(row_count, dtype=jnp.int32)) // rows_per
    keep = jnp.take(block_pattern[0], row_ids).astype(jnp.bfloat16)
    masked = factor_block * keep[None, :, None]
    ancestor_part = lax.all_gather(ancestor_inverse, "leaf", axis=1, tiled=True)
    product = jnp.dot(
        ancestor_part,
        lax.all_gather(masked, "grid", axis=1, tiled=True)[0],
        preferred_element_type=jnp.float32,
    )
    cross = -product
    partial_terms = jnp.sum(masked[0].astype(jnp.float32) * cross, axis=0)
    summed = lax.psum_scatter(partial_terms, "grid", scatter_dimension=0, tiled=True)
    variance = pivot_inverse[0] - summed
    cross_cov = cross.astype(jnp.bfloat16)[None]
    return (cross_cov, variance[None])


def solution(mesh):
    return jax.shard_map(
        on_device,
        mesh=mesh,
        in_specs=(P("grid", "leaf"), P("leaf", "grid", None), P("leaf", None), P("leaf", "grid")),
        out_specs=(P("leaf", "grid", None), P("leaf", "grid")),
        check_vma=False,
    )
```

profile of v0, /device:TPU:1, one launch (start us, length us, event | category | flops | bytes accessed | tf_op | source)
XLA Modules:
  0.0 199.4 jit_solution(11581018325213134794)
XLA Ops:
  7.2 0.0 copy-start
  7.2 0.0 all-gather.2.cloned.1.call-start
  7.2 2.0 fusion.11
  9.2 9.9 %fusion.10 = bf16[128]{0:T(256)(128)(2,1)S(1)} fusion(s32[]{:T(128)} %bitcast.18, s32[]{:T(128)} %bitcast.19, s32[]{:T(128)} %bitcast.20, s32[]{:T(128)} %bitcast.21, s32[]{:T(128)} %bitcast.22, s32[]{:T(128)} %bitcast.24, s32[]{:T(128)} %bitcast.23, s32[]{:T(128)} %bitcast.1, s32[]{:T(128)} %bitcast.3, s32[]{:T(128)} %bitcast.5, s32[]{:T(128)} %bitcast.7, ...), kind=kLoop, calls=%fused_computation.36 | loop fusion | flops 9344 | bytes 324 | tf_op jit(solution)/shard_map/convert_element_type | solution.py:13
  19.1 2.3 %broadcast_multiply_fusion = bf16[1,128,4096]{2,1,0:T(8,128)(2,1)} fusion(bf16[1,128,4096]{2,1,0:T(8,128)(2,1)} %param.5, bf16[128]{0:T(256)(128)(2,1)S(1)} %fusion.10), kind=kLoop, calls=%fused_computation.7 | loop fusion | flops 524288 | bytes 2097408 | tf_op jit(solution)/shard_map/mul | solution.py:14
  21.4 0.0 all-gather.2.cloned.1.call-update
  21.5 1.3 dynamic-slice
  23.4 73.6 %all_gather.7 = bf16[128,2048]{0,1:T(8,128)(2,1)S(1)} all-gather(bf16[128,64]{0,1:T(8,128)(2,1)} %param.4), channel_id=1, replica_groups=mesh['leaf'=32,'grid'=16] {'leaf'}, dimensions={1}, use_global_device_ids=true | all-gather | bytes 540672 | tf_op jit(solution)/shard_map/all_gather | solution.py:15
  97.0 34.2 %all-gather.2.cloned.1.call-done = bf16[1,2048,4096]{2,1,0:T(8,128)(2,1)} async-done(((bf16[1,128,4096]{2,1,0:T(8,128)(2,1)}), bf16[1,2048,4096]{2,1,0:T(8,128)(2,1)}) %all-gather.2.cloned.1.call-update) | async-done | bytes 16777232 | tf_op jit(solution)/shard_map/all_gather | solution.py:18
  131.2 9.6 %fusion.8 = (f32[4096]{0:T(1024)S(1)}, bf16[1,128,4096]{2,1,0:T(8,128)(2,1)}) fusion(bf16[1,128,4096]{2,1,0:T(8,128)(2,1)} %broadcast_multiply_fusion, bf16[128,2048]{0,1:T(8,128)(2,1)S(1)} %all_gather.7, bf16[1,2048,4096]{2,1,0:T(8,128)(2,1)} %all-gather.2.cloned.1.call-done), kind=kOutput, calls=%fused_computation.5 | convolution fusion | flops 2150100992 | bytes 19415040 | tf_op jit(solution)/shard_map/dot_general | solution.py:16
  140.8 51.2 %all-reduce = f32[4096]{0:T(1024)S(1)} all-reduce(f32[4096]{0:T(1024)S(1)} %get-tuple-element.2), channel_id=2, replica_groups=mesh['leaf'=32,'grid'=16] {'grid'}, use_global_device_ids=true, to_apply=%region_1.2.clone | all-reduce | flops 4096 | bytes 32768
  191.9 0.0 copy-done
  191.9 0.6 dynamic-slice_subtract_fusion
Async XLA Ops:
  7.2 184.7 %copy-start = (f32[1,256]{1,0:T(1,128)S(1)}, f32[1,256]{1,0:T(1,128)}, u32[]{:S(2)}) copy-start(f32[1,256]{1,0:T(1,128)} %param.7) | copy-start | bytes 3076
  7.2 124.0 %all-gather.2.cloned.1.call-start = ((), (), s32[]{:S(2)}) async-start(), calls=%async_computation | async-start | bytes 17825792 | tf_op jit(solution)/shard_map/all_gather | solution.py:18
Sparse Core Ops, SparseCore 0:
  21.6 109.5 all-gather.1
where the time goes:
time: 203 us; the launch traced here: 199 us
  blocking collectives  125 us (62%)
  waiting for transfers between devices  34.2 us (17%)
  between operations  14.7 us (7%)
  other arithmetic  12.9 us (6%)
  matrix products  9.58 us (5%)
  local copies, waits for them, and re-layouts  3.23 us (2%)
    all_gather x1, blocking collectives, on_device(): ancestor_part = lax.all_gather(ancestor_inverse, 'leaf', axis=1, tiled=True)  73.6 us
    unnamed x1, blocking collectives  51.2 us
    all_gather x1, waiting for transfers between devices, on_device(): lax.all_gather(masked, 'grid', axis=1, tiled=True)[0]  34.2 us
    convert_element_type x1, other arithmetic, on_device(): keep = jnp.take(block_pattern[0], row_ids).astype(jnp.bfloat16)  9.92 us
    dot_general x1, matrix products, on_device(): jnp.dot(ancestor_part, lax.all_gather(masked, 'grid', axis=1, tiled=True)...  9.58 us
  transfers between devices with their start and end apart: 1, of which 1 were waited for; matrix products, arithmetic and copies ran while one was open for 1% of the time, Pallas kernels for 0%

commit v1 on v0

v1 whole, which is shorter than its diff:
```python
import jax
import jax.numpy as jnp
from jax import lax
from jax.experimental import pallas as pl
from jax.experimental.pallas import tpu as pltpu
from jax.sharding import PartitionSpec as P

MESH = pl.DeviceIdType.MESH
F32, BF16 = jnp.float32, jnp.bfloat16
NX, NY, NC, NZ = 2, 4, 2, 16
ROWS, SEG = 128, 256
AHEAD = 1
PASSES = (2, 1, 3, 0)


def kernel(
    a_ref, f_ref, pat_ref, piv_ref, out_ref, var_ref,
    raw, masked, anc, place, got, cov, vpart, vgot,
    m_send, x_send, m_recv, m_local, h_sem, t_send, t_recv,
    z_send, z_recv, c_send, c_recv, o_send, o_recv, o_local, v_sem,
):
    leaf, grid = lax.axis_index("leaf"), lax.axis_index("grid")
    xh, z = leaf // NZ, lax.rem(leaf, NZ)
    x, y, c = grid // (NY * NC), lax.rem(grid // NC, NY), lax.rem(grid, NC)

    def around_y(dy):
        return lax.rem(y + dy, NY)

    def around_z(dz):
        return lax.rem(z + dz + NZ, NZ)

    def core(dc):
        return lax.rem(c + dc, NC)

    def here(dy, dc):
        return (leaf, x * NY * NC + around_y(dy) * NC + core(dc))

    x_mate = (leaf, (1 - x) * NY * NC + y * NC + c)
    h_mate = ((1 - xh) * NZ + z, grid)
    z_next = (xh * NZ + around_z(1), grid)
    z_prev = (xh * NZ + around_z(-1), grid)

    def block(dy, dc):
        return around_y(dy) * NC + core(dc)

    def columns(s, b):
        return pl.ds(pl.multiple_of(s * NY * NC * SEG + b * SEG, SEG), SEG)

    others = [(dy, dc) for dy in (2, 1, 3) for dc in range(NC)] + [(0, 1)]
    sends = []

    def remote(src, dst, send, recv, to):
        return pltpu.make_async_remote_copy(
            src_ref=src, dst_ref=dst, send_sem=send, recv_sem=recv, device_id=to, device_id_type=MESH
        )

    def send(*copy):
        handle = remote(*copy)
        handle.start()
        sends.append(handle)

    barrier = pltpu.get_barrier_semaphore()
    known = [here(dy, dc) for dy, dc in others] + [x_mate, h_mate, z_next, z_prev]
    for to in known:
        pl.semaphore_signal(barrier, inc=1, device_id=to, device_id_type=MESH)
    own = a_ref[...]
    nil = jnp.zeros_like(own)
    place[...] = jnp.where(xh == 0, jnp.concatenate([own, nil], 1), jnp.concatenate([nil, own], 1))
    pl.semaphore_wait(barrier, len(known))

    h_copy = remote(place, got, h_sem.at[0], h_sem.at[1], h_mate)
    h_copy.start()

    me = block(0, 0)

    def slot(s, b, side):
        return raw.at[s, b, :, side]

    def scatter(s):
        mine = f_ref.at[:, :, columns(s, me)]
        send(mine, slot(s, me, x), x_send.at[s, 0], m_recv.at[s, x, me], x_mate)
        for k, (dy, dc) in enumerate(others):
            part = f_ref.at[:, :, columns(s, block(dy, dc))]
            send(part, slot(s, me, x), m_send.at[s, k], m_recv.at[s, x, me], here(dy, dc))
        local = pltpu.make_async_copy(mine, slot(s, me, x), m_local.at[s])
        local.start()
        return local

    def arrived(s, b, side):
        remote(slot(s, b, side), slot(s, b, side), x_send.at[s, 0], m_recv.at[s, side, b], x_mate).wait_recv()

    def pass_over(s, k):
        b = block(*others[k])
        arrived(s, b, x)
        send(slot(s, b, x), slot(s, b, x), x_send.at[s, k + 1], m_recv.at[s, x, b], x_mate)

    locals_ = [scatter(0)]

    h_copy.wait()
    anc[z, y, c] = place[...] + got[...]

    def ring(step, p, way, to):
        q = around_y(PASSES[p])
        part = anc.at[around_z(-step if way == 0 else step), q, c]
        send(part, part, z_send.at[way, step, p], z_recv.at[way, step, p], to)

    def to_core(origin, p):
        part = anc.at[around_z(-origin), around_y(PASSES[p]), c]
        send(part, part, c_send.at[origin % NZ, p], c_recv.at[origin % NZ, p], here(0, 1))

    def ring_both(p):
        ring(0, p, 0, z_next)
        ring(0, p, 1, z_prev)
        to_core(0, p)

    mine = anc.at[z, y, c]
    for k, dy in enumerate((2, 1, 3)):
        send(mine, mine, t_send.at[k], t_recv.at[dy], here(dy, 0))
    ring_both(PASSES.index(0))
    locals_.append(scatter(1))
    for dy in (1, 3, 2):
        part = anc.at[z, around_y(dy), c]
        remote(part, part, t_send.at[0], t_recv.at[NY - dy], here(dy, 0)).wait_recv()
        ring_both(PASSES.index(dy))

    for k in (6, 2, 3, 4, 5, 0, 1):
        pass_over(0, k)

    def ring_step(step, p):
        q = around_y(PASSES[p])
        for way, to in ((0, z_next), (1, z_prev)):
            if step == NZ // 2 and way != p % 2:
                continue
            origin = step if way == 0 else -step
            part = anc.at[around_z(-origin), q, c]
            remote(part, part, z_send.at[way, 0, p], z_recv.at[way, step - 1, p], to).wait_recv()
            if step < NZ // 2 - 1 or (step == NZ // 2 - 1 and way == p % 2):
                ring(step, p, way, to)
            to_core(origin, p)

    def mask(s):
        locals_[s].wait()
        for b in range(NY * NC):
            for side in range(NX):
                keep = jnp.full((2, 64, SEG), pat_ref[0, side * NY * NC + b].astype(F32), F32).astype(BF16)
                masked[s, b, :, side] = raw[s, b, :, side] * keep

    def gathered(s):
        for dy in range(NY):
            for dc in range(NC):
                arrived(s, block(dy, dc), 1 - x)
        mask(s)

    def pass_done(p):
        for origin in range(NZ):
            part = anc.at[around_z(-origin), around_y(PASSES[p]), core(1)]
            remote(part, part, c_send.at[0, p], c_recv.at[origin, p], here(0, 1)).wait_recv()

    def product(s, p):
        q = around_y(PASSES[p])
        total = jnp.zeros((NC * ROWS, SEG), F32)
        for k in range(NZ // 2):
            left = jnp.concatenate(
                [anc[2 * k, q].reshape(NC * ROWS, 128), anc[2 * k + 1, q].reshape(NC * ROWS, 128)], 1
            )
            total += jnp.dot(left, masked[s, k].reshape(256, SEG), preferred_element_type=F32)
        cross = -total
        rows = jnp.concatenate([masked[s, NC * q + cc, :, x].reshape(ROWS, SEG) for cc in range(NC)], 0)
        terms = rows.astype(F32) * cross
        vpart[s] += jnp.sum(terms.reshape(NC * ROWS // 8, 8, SEG), axis=0)
        cov[s, p] = cross.astype(BF16).reshape(NC, ROWS, SEG)
        for dc in range(NC):
            part, there = cov.at[s, p, core(dc)], out_ref.at[:, columns(s, me)]
            if PASSES[p] == 0 and dc == 0:
                pltpu.make_async_copy(part, there, o_local.at[s]).start()
            else:
                k = others.index((PASSES[p], dc))
                send(part, there, o_send.at[s, k], o_recv.at[s, k], here(PASSES[p], dc))

    vpart[...] = jnp.zeros_like(vpart)
    ticks = NZ // 2 + AHEAD * (NY - 1)
    left = {0: [(1, 6), (1, 2), (1, 3)], 1: [(1, 4), (1, 5)], 2: [(1, 0), (1, 1)]}
    ready = False
    for t in range(ticks):
        for p in range(NY):
            step = t - AHEAD * p + 1
            if 1 <= step <= NZ // 2:
                ring_step(step, p)
        for s, k in left.get(t, []):
            pass_over(s, k)
        p, late = divmod(t - (NZ // 2 - 1), AHEAD)
        if 0 <= p < NY and late == 0:
            if not ready:
                gathered(0)
                ready = True
            pass_done(p)
            product(0, p)
    gathered(1)
    for p in range(NY):
        product(1, p)

    v_copy = remote(vpart.at[1 - x], vgot, v_sem.at[0], v_sem.at[1], x_mate)
    v_copy.start()
    for s in range(NX):
        for k, (dy, dc) in enumerate(others):
            k_back = others.index(((NY - dy) % NY, dc))
            there = out_ref.at[:, columns(s, block(dy, dc))]
            remote(cov.at[s, 0, 0], there, o_send.at[s, 0], o_recv.at[s, k_back], here(dy, dc)).wait_recv()
        pltpu.make_async_copy(cov.at[s, 0, 0], out_ref.at[:, columns(s, me)], o_local.at[s]).wait()
    v_copy.wait()
    total = jnp.sum(vpart[x] + vgot[...], axis=0, keepdims=True)
    var_ref[...] = piv_ref[...] - total
    for handle in sends:
        handle.wait_send()


def on_device(ancestor_inverse, factor_block, block_pattern, pivot_inverse):
    rows, wide = factor_block.shape[1:]
    dma = pltpu.SemaphoreType.DMA
    vmem, hbm = pl.BlockSpec(memory_space=pltpu.VMEM), pl.BlockSpec(memory_space=pl.ANY)
    cross_cov, variances = pl.pallas_call(
        kernel,
        out_shape=(
            jax.ShapeDtypeStruct((rows, wide), BF16),
            jax.ShapeDtypeStruct(pivot_inverse.shape, F32),
        ),
        in_specs=[vmem, hbm, pl.BlockSpec(memory_space=pltpu.SMEM), vmem],
        out_specs=(hbm, vmem),
        scratch_shapes=[
            pltpu.VMEM((NX, NY * NC, 2, NX, 64, SEG), BF16),
            pltpu.VMEM((NX, NY * NC, 2, NX, 64, SEG), BF16),
            pltpu.VMEM((NZ, NY, NC, ROWS, 128), BF16),
            pltpu.VMEM((ROWS, 128), BF16),
            pltpu.VMEM((ROWS, 128), BF16),
            pltpu.VMEM((NX, NY, NC, ROWS, SEG), BF16),
            pltpu.VMEM((NX, 8, SEG), F32),
            pltpu.VMEM((8, SEG), F32),
            dma((NX, 7)), dma((NX, 8)), dma((NX, NX, 8)), dma((NX,)),
            dma((2,)), dma((3,)), dma((4,)),
            dma((2, NZ // 2, NY)), dma((2, NZ // 2, NY)),
            dma((NZ, NY)), dma((NZ, NY)),
            dma((NX, 7)), dma((NX, 7)), dma((NX,)), dma((2,)),
        ],
        compiler_params=pltpu.CompilerParams(
            collective_id=0, has_side_effects=True, vmem_limit_bytes=48 << 20
        ),
    )(ancestor_inverse, factor_block.reshape(2, rows // 2, wide), block_pattern, pivot_inverse)
    return cross_cov[None], variances


def solution(mesh):
    return jax.shard_map(
        on_device,
        mesh=mesh,
        in_specs=(P("grid", "leaf"), P("leaf", "grid", None), P("leaf", None), P("leaf", "grid")),
        out_specs=(P("leaf", "grid", None), P("leaf", "grid")),
        check_vma=False,
    )
```

time: 203 us -> 82.2 us (0.40); the launches traced: 199 us -> 82 us
  blocking collectives: 125 us -> 0 us
  Pallas kernels: 0 us -> 77.7 us
  waiting for transfers between devices: 34.2 us -> 0 us
  between operations: 14.7 us -> 0.68 us
  other arithmetic: 12.9 us -> 0 us
  matrix products: 9.58 us -> 0 us
    pallas_call x0 -> x1, Pallas kernels: none -> 77.7 us  [on_device(): pl.pallas_call(kernel, out_shape=(jax.ShapeDtypeStruct((rows, wide), BF16...]
    all_gather x1 -> x0, blocking collectives: 73.6 us -> none  [on_device(): ancestor_part = lax.all_gather(ancestor_inverse, 'leaf', axis=1, tiled=True)]
    unnamed x1 -> x0, blocking collectives: 51.2 us -> none
    all_gather x1 -> x0, waiting for transfers between devices: 34.2 us -> none  [on_device(): lax.all_gather(masked, 'grid', axis=1, tiled=True)[0]]
    convert_element_type x1 -> x0, other arithmetic: 9.92 us -> none  [on_device(): keep = jnp.take(block_pattern[0], row_ids).astype(jnp.bfloat16)]
    dot_general x1 -> x0, matrix products: 9.58 us -> none  [on_device(): jnp.dot(ancestor_part, lax.all_gather(masked, 'grid', axis=1, tiled=True)...]
    mul x1 -> x0, other arithmetic: 2.33 us -> none  [on_device(): masked = factor_block * keep[None, :, None]]
    unnamed x3 -> x9, local copies, waits for them, and re-layouts: 1.27 us -> 3.6 us
  transfers between devices with their start and end apart: 1 -> 0, of which waited for: 1 -> 0; matrix products, arithmetic and copies ran while one was open for 1% -> 0% of each run, Pallas kernels for 0% -> 0%
where the time goes in v1:
time: 82.2 us; the launch traced here: 82 us
  Pallas kernels  77.7 us (95%)
  local copies, waits for them, and re-layouts  3.6 us (4%)
    pallas_call x1, Pallas kernels, on_device(): pl.pallas_call(kernel, out_shape=(jax.ShapeDtypeStruct((rows, wide), BF16...  77.7 us
    unnamed x9, local copies, waits for them, and re-layouts  3.6 us

profile of v1, /device:TPU:1, one launch (start us, length us, event | category | flops | bytes accessed | tf_op | source)
XLA Modules:
  0.0 82.0 jit_solution(11174070878702536397)
XLA Ops:
  0.6 0.0 copy-start.1
  0.6 0.0 copy-start.2
  0.6 0.8 %copy.6.a_ref = bf16[128,64]{1,0:T(8,128)(2,1)S(1)} copy(bf16[128,64]{0,1:T(8,128)(2,1)} %param.4) | data formatting | bytes 32768 | tf_op args[0]
  1.5 0.0 copy-done.1
  1.5 0.0 copy-done.2
  1.5 0.0 copy-start
  1.5 1.2 %copy-done = bf16[1,128,4096]{2,1,0:T(8,128)(2,1)S(1)} copy-done((bf16[1,128,4096]{2,1,0:T(8,128)(2,1)S(1)}, bf16[1,128,4096]{2,1,0:T(8,128)(2,1)}, u32[]{:S(2)}) %copy-start) | copy-done | bytes 1048600
  2.7 77.7 %shard_map.59 = (bf16[128,4096]{1,0:T(8,128)(2,1)S(1)}, f32[1,256]{1,0:T(1,128)S(1)}) custom-call(bf16[128,64]{1,0:T(8,128)(2,1)S(1)} %copy.6.a_ref, bf16[2,64,4096]{2,1,0:T(8,128)(2,1)S(1)} %bitcast.2, s32[1,16]{1,0:T(1,128)S(1)} %copy-done.2, f32[1,256]{1,0:T(1,128)S(1)} %copy-done.1), custom_call_target="tpu_custom_call" | custom-call | tf_op jit(solution)/shard_map/pallas_call | solution.py:221
  80.5 1.0 %copy.9 = bf16[1,128,4096]{2,1,0:T(8,128)(2,1)} copy(bf16[1,128,4096]{2,1,0:T(8,128)(2,1)S(1)} %bitcast.3) | data formatting | bytes 2097152
  81.4 0.6 copy.10
Async XLA Ops:
  0.6 0.9 %copy-start.1 = (f32[1,256]{1,0:T(1,128)S(1)}, f32[1,256]{1,0:T(1,128)}, u32[]{:S(2)}) copy-start(f32[1,256]{1,0:T(1,128)} %piv_ref.1) | copy-start | bytes 3076
  0.6 0.9 %copy-start.2 = (s32[1,16]{1,0:T(1,128)S(1)}, s32[1,16]{1,0:T(1,128)}, u32[]{:S(2)}) copy-start(s32[1,16]{1,0:T(1,128)} %pat_ref.1) | copy-start | bytes 196
  1.5 1.2 %copy-start = (bf16[1,128,4096]{2,1,0:T(8,128)(2,1)S(1)}, bf16[1,128,4096]{2,1,0:T(8,128)(2,1)}, u32[]{:S(2)}) copy-start(bf16[1,128,4096]{2,1,0:T(8,128)(2,1)} %param.5) | copy-start | bytes 3145732

commit v2 on v0

v2 whole, which is shorter than its diff:
```python
import jax
import jax.numpy as jnp
from jax import lax
from jax.experimental import pallas as pl
from jax.experimental.pallas import tpu as pltpu
from jax.sharding import PartitionSpec as P

MESH = pl.DeviceIdType.MESH
F32, BF16 = jnp.float32, jnp.bfloat16
NX, NY, NC, NZ = 2, 4, 2, 16
ROWS, SEG = 128, 256
CHUNKS = 4
DEEP = 1024
FAR = 4


def kernel(
    a_ref, f_ref, pat_ref, piv_ref, out_ref, var_ref,
    raw, masked, anc, own, packed, cov, vpart, vgot,
    a_sem, s_send, s_recv, l_sem, y_send, y_recv, w_send, w_recv,
    z_send, z_recv, x_send, x_recv, o_send, o_recv, o_local, v_send, v_recv,
):
    leaf, grid = lax.axis_index("leaf"), lax.axis_index("grid")
    xh, z = leaf // NZ, lax.rem(leaf, NZ)
    x, y, c = grid // (NY * NC), lax.rem(grid // NC, NY), lax.rem(grid, NC)
    place_x = xh * NX + x

    def up_y(dy):
        return lax.rem(y + dy, NY)

    def up_z(dz):
        return lax.rem(z + dz + NZ, NZ)

    def other(v, d):
        return lax.rem(v + d, 2)

    def group(dx, dy, dc):
        return (leaf, other(x, dx) * NY * NC + up_y(dy) * NC + other(c, dc))

    def along_z(dz):
        return (xh * NZ + up_z(dz), grid)

    def chip_x(d):
        at = lax.rem(place_x + d, 2 * NX)
        return at // NX, lax.rem(at, NX)

    def along_x(d):
        h, low = chip_x(d)
        return (h * NZ + z, low * NY * NC + y * NC + c)

    core_mate = group(0, 0, 1)
    square = [(0, 1), (1, 0), (1, 1)]
    steps_z = [s * d for d in range(1, FAR + 1) for s in (1, -1)]
    sends = []

    def remote(src, dst, send, recv, to):
        return pltpu.make_async_remote_copy(
            src_ref=src, dst_ref=dst, send_sem=send, recv_sem=recv, device_id=to, device_id_type=MESH
        )

    def send(*copy):
        handle = remote(*copy)
        handle.start()
        sends.append(handle)

    def wait(ref, sem):
        remote(ref, ref, a_sem, sem, core_mate).wait_recv()

    def columns(side, t, cc):
        return pl.ds(pl.multiple_of(((side * NY + t) * NC + cc) * SEG, SEG), SEG)

    a_copy = pltpu.make_async_copy(a_ref, own, a_sem)
    a_copy.start()
    known = [group(dx, 0, dc) for dx, dc in square] + [group(0, dy, 0) for dy in (1, 2, 3)]
    known += [along_x(3 - 2 * xo) for xo in ()] + [along_z(d) for d in steps_z]
    outer = lax.rem(place_x + jnp.where(x == 0, 3, 1), 2 * NX)
    outer_id = ((outer // NX) * NZ + z, lax.rem(outer, NX) * NY * NC + y * NC + c)
    known.append(outer_id)
    barrier = pltpu.get_barrier_semaphore()
    for to in known:
        pl.semaphore_signal(barrier, inc=1, device_id=to, device_id_type=MESH)
    a_copy.wait()
    packed[z] = jnp.concatenate([own[: ROWS // 2], own[ROWS // 2 :]], 1)
    pl.semaphore_wait(barrier, len(known))

    def way(d):
        return (0, d - 1) if d > 0 else (1, -d - 1)

    def send_z(origin, d):
        to = way(d - origin)
        send(packed.at[up_z(origin)], packed.at[up_z(origin)], z_send.at[*to], z_recv.at[*to], along_z(d))

    def wait_z(d):
        wait(packed.at[up_z(-d)], z_recv.at[*way(d)])

    for d in reversed(steps_z):
        send_z(0, d)

    def swap(t):
        mine = raw.at[t, x, y, c]
        for k, (dx, dc) in enumerate(square):
            part = f_ref.at[:, columns(other(x, dx), t, other(c, dc))]
            send(part, mine, s_send.at[t, k], s_recv.at[t, k], group(dx, 0, dc))
        local = pltpu.make_async_copy(f_ref.at[:, columns(x, t, c)], mine, l_sem.at[t])
        local.start()
        return local

    def spread(t, local):
        local.wait()
        for dx in range(NX):
            side = other(x, dx)
            for k, (ddx, dc) in enumerate(square):
                if ddx == dx:
                    wait(raw.at[t, side, y, other(c, dc)], s_recv.at[t, k])
            both = raw.at[t, side, y]
            for k, dy in enumerate((1, 3)):
                send(both, both, y_send.at[t, k, side], y_recv.at[t, k, side], group(0, dy, 0))

    def hand_on(t):
        for k, dy in enumerate((1, 3)):
            for dx in (k, 1 - k):
                part = raw.at[t, dx, up_y(NY - dy)]
                wait(part, y_recv.at[t, k, dx])
                if dx == k:
                    send(part, part, w_send.at[t, k], w_recv.at[t, k], group(0, dy, 0))

    def complete(t):
        for k in range(2):
            wait(raw.at[t, k, up_y(2)], w_recv.at[t, k])

    swaps = [swap(0), swap(1)]
    spread(0, swaps[0])
    swaps.append(swap(2))

    wait_z(FAR)
    for d in range(FAR, 0, -1):
        send_z(-FAR, d)
    wait_z(-FAR)
    for d in range(1 - FAR, 0):
        send_z(FAR, d)

    spread(1, swaps[1])
    swaps.append(swap(3))
    hand_on(0)

    for d in range(1, NZ // 2 + 1):
        for s in (1, -1):
            if d != FAR and s * d != -NZ // 2:
                wait_z(s * d)
    for k in range(NZ // 2):
        even, odd = packed[2 * k], packed[2 * k + 1]
        for half in range(2):
            lanes = slice(half * 64, half * 64 + 64)
            anc[xh, x, c, half * 64 : half * 64 + 64, k * 128 : k * 128 + 128] = jnp.concatenate(
                [even[:, lanes], odd[:, lanes]], 1
            )

    mine = anc.at[xh, x, c]
    for k, d in enumerate((1, 3)):
        send(mine, mine, x_send.at[k], x_recv.at[k], along_x(d))
    send(mine, mine, x_send.at[2], x_recv.at[2], core_mate)

    spread(2, swaps[2])
    hand_on(1)

    for k, d in enumerate((1, 3)):
        h, low = chip_x(2 * NX - d)
        part = anc.at[h, low, c]
        wait(part, x_recv.at[k])
        some = part.at[k * 64 : k * 64 + 64]
        send(some, some, x_send.at[3 + k], x_recv.at[3 + k], along_x(d))
        send(part, part, x_send.at[5 + k], x_recv.at[5 + k], core_mate)
    spread(3, swaps[3])
    h, low = chip_x(2)
    for k in range(2):
        some = anc.at[h, low, c, k * 64 : k * 64 + 64]
        wait(some, x_recv.at[3 + k])
        send(some, some, x_send.at[7 + k], x_recv.at[7 + k], core_mate)
    hand_on(2)
    wait(anc.at[xh, x, other(c, 1)], x_recv.at[2])
    for k, d in enumerate((1, 3)):
        hh, ll = chip_x(2 * NX - d)
        wait(anc.at[hh, ll, other(c, 1)], x_recv.at[5 + k])
    for k in range(2):
        wait(anc.at[h, low, other(c, 1), k * 64 : k * 64 + 64], x_recv.at[7 + k])

    def product(t):
        def keep_block(g, _):
            keep = jnp.full((ROWS, SEG), pat_ref[0, g].astype(F32), F32).astype(BF16)
            side, yy, cc = g // (NY * NC), lax.rem(g // NC, NY), lax.rem(g, NC)
            masked[side, yy, cc] = raw[t, side, yy, cc] * keep
            return 0

        lax.fori_loop(0, NX * NY * NC, keep_block, 0)
        vpart[t] = jnp.zeros((8, SEG), F32)

        def rows_of(i, _):
            side, cc = i // NC, lax.rem(i, NC)
            total = jnp.zeros((ROWS, SEG), F32)
            for k in range(NX):
                total += jnp.dot(anc[k, side, cc], masked[k].reshape(DEEP, SEG), preferred_element_type=F32)
            cross = -total
            terms = masked[side, y, cc].astype(F32) * cross
            vpart[t] += jnp.sum(terms.reshape(ROWS // 8, 8, SEG), axis=0)
            cov[t, side, cc] = cross.astype(BF16)
            return 0

        lax.fori_loop(0, NX * NC, rows_of, 0)
        there = out_ref.at[:, columns(x, t, c)]
        for k, (dx, dc) in enumerate(square):
            part = cov.at[t, other(x, dx), other(c, dc)]
            send(part, there, o_send.at[t, k], o_recv.at[t, k], group(dx, 0, dc))
        pltpu.make_async_copy(cov.at[t, x, c], there, o_local.at[t]).start()

    for t in range(CHUNKS):
        if t == CHUNKS - 1:
            hand_on(t)
        complete(t)
        product(t)

    for k, dy in enumerate((1, 2, 3)):
        send(vpart.at[up_y(dy)], vgot.at[k], v_send.at[k], v_recv.at[k], group(0, dy, 0))
    for t in range(CHUNKS):
        for k, (dx, dc) in enumerate(square):
            wait(out_ref.at[:, columns(other(x, dx), t, other(c, dc))], o_recv.at[t, k])
        there = out_ref.at[:, columns(x, t, c)]
        pltpu.make_async_copy(cov.at[t, x, c], there, o_local.at[t]).wait()
    total = vpart[y]
    for k in range(3):
        wait(vgot.at[k], v_recv.at[k])
        total += vgot[k]
    var_ref[...] = piv_ref[...] - jnp.sum(total, axis=0, keepdims=True)
    for handle in sends:
        handle.wait_send()


def on_device(ancestor_inverse, factor_block, block_pattern, pivot_inverse):
    rows, wide = factor_block.shape[1:]
    dma = pltpu.SemaphoreType.DMA
    vmem, hbm = pl.BlockSpec(memory_space=pltpu.VMEM), pl.BlockSpec(memory_space=pltpu.HBM)
    cross_cov, variances = pl.pallas_call(
        kernel,
        out_shape=(
            jax.ShapeDtypeStruct((rows, wide), BF16),
            jax.ShapeDtypeStruct(pivot_inverse.shape, F32),
        ),
        in_specs=[hbm, hbm, pl.BlockSpec(memory_space=pltpu.SMEM), vmem],
        out_specs=(hbm, vmem),
        scratch_shapes=[
            pltpu.VMEM((CHUNKS, NX, NY, NC, ROWS, SEG), BF16),
            pltpu.VMEM((NX, NY, NC, ROWS, SEG), BF16),
            pltpu.VMEM((2, NX, NC, ROWS, DEEP), BF16),
            pltpu.VMEM((ROWS, 64), BF16),
            pltpu.VMEM((NZ, ROWS // 2, 128), BF16),
            pltpu.VMEM((CHUNKS, NX, NC, ROWS, SEG), BF16),
            pltpu.VMEM((CHUNKS, 8, SEG), F32),
            pltpu.VMEM((3, 8, SEG), F32),
            dma, dma((CHUNKS, 3)), dma((CHUNKS, 3)), dma((CHUNKS,)),
            dma((CHUNKS, 2, 2)), dma((CHUNKS, 2, 2)), dma((CHUNKS, 2)), dma((CHUNKS, 2)),
            dma((2, 8)), dma((2, 8)), dma((9,)), dma((9,)),
            dma((CHUNKS, 3)), dma((CHUNKS, 3)), dma((CHUNKS,)), dma((3,)), dma((3,)),
        ],
        compiler_params=pltpu.CompilerParams(
            collective_id=0, has_side_effects=True, vmem_limit_bytes=48 << 20
        ),
    )(ancestor_inverse, factor_block[0], block_pattern, pivot_inverse)
    return cross_cov[None], variances


def solution(mesh):
    return jax.shard_map(
        on_device,
        mesh=mesh,
        in_specs=(P("grid", "leaf"), P("leaf", "grid", None), P("leaf", None), P("leaf", "grid")),
        out_specs=(P("leaf", "grid", None), P("leaf", "grid")),
        check_vma=False,
    )
```

time: 203 us -> 67.7 us (0.33); the launches traced: 199 us -> 67.5 us
  blocking collectives: 125 us -> 0 us
  Pallas kernels: 0 us -> 63.2 us
  waiting for transfers between devices: 34.2 us -> 0 us
  between operations: 14.7 us -> 0.68 us
  other arithmetic: 12.9 us -> 0 us
  matrix products: 9.58 us -> 0 us
    all_gather x1 -> x0, blocking collectives: 73.6 us -> none  [on_device(): ancestor_part = lax.all_gather(ancestor_inverse, 'leaf', axis=1, tiled=True)]
    pallas_call x0 -> x1, Pallas kernels: none -> 63.2 us  [on_device(): pl.pallas_call(kernel, out_shape=(jax.ShapeDtypeStruct((rows, wide), BF16...]
    unnamed x1 -> x0, blocking collectives: 51.2 us -> none
    all_gather x1 -> x0, waiting for transfers between devices: 34.2 us -> none  [on_device(): lax.all_gather(masked, 'grid', axis=1, tiled=True)[0]]
    convert_element_type x1 -> x0, other arithmetic: 9.92 us -> none  [on_device(): keep = jnp.take(block_pattern[0], row_ids).astype(jnp.bfloat16)]
    dot_general x1 -> x0, matrix products: 9.58 us -> none  [on_device(): jnp.dot(ancestor_part, lax.all_gather(masked, 'grid', axis=1, tiled=True)...]
    mul x1 -> x0, other arithmetic: 2.33 us -> none  [on_device(): masked = factor_block * keep[None, :, None]]
    unnamed x3 -> x9, local copies, waits for them, and re-layouts: 1.27 us -> 3.6 us
  transfers between devices with their start and end apart: 1 -> 0, of which waited for: 1 -> 0; matrix products, arithmetic and copies ran while one was open for 1% -> 0% of each run, Pallas kernels for 0% -> 0%
where the time goes in v2:
time: 67.7 us; the launch traced here: 67.5 us
  Pallas kernels  63.2 us (93%)
  local copies, waits for them, and re-layouts  3.6 us (5%)
  between operations  0.68 us (1%)
    pallas_call x1, Pallas kernels, on_device(): pl.pallas_call(kernel, out_shape=(jax.ShapeDtypeStruct((rows, wide), BF16...  63.2 us
    unnamed x9, local copies, waits for them, and re-layouts  3.6 us

profile of v2, /device:TPU:1, one launch (start us, length us, event | category | flops | bytes accessed | tf_op | source)
XLA Modules:
  0.0 67.5 jit_solution(4083883425114285214)
XLA Ops:
  0.6 0.0 copy-start.1
  0.6 0.0 copy-start.2
  0.6 0.8 %copy.6.a_ref = bf16[128,64]{1,0:T(8,128)(2,1)S(1)} copy(bf16[128,64]{0,1:T(8,128)(2,1)} %param.4) | data formatting | bytes 32768 | tf_op args[0]
  1.5 0.0 copy-done.1
  1.5 0.0 copy-done.2
  1.5 0.0 copy-start
  1.5 1.2 %copy-done = bf16[1,128,4096]{2,1,0:T(8,128)(2,1)S(1)} copy-done((bf16[1,128,4096]{2,1,0:T(8,128)(2,1)S(1)}, bf16[1,128,4096]{2,1,0:T(8,128)(2,1)}, u32[]{:S(2)}) %copy-start) | copy-done | bytes 1048600
  2.7 63.2 %shard_map.59 = (bf16[128,4096]{1,0:T(8,128)(2,1)S(1)}, f32[1,256]{1,0:T(1,128)S(1)}) custom-call(bf16[128,64]{1,0:T(8,128)(2,1)S(1)} %copy.6.a_ref, bf16[128,4096]{1,0:T(8,128)(2,1)S(1)} %bitcast.2, s32[1,16]{1,0:T(1,128)S(1)} %copy-done.2, f32[1,256]{1,0:T(1,128)S(1)} %copy-done.1), custom_call_target="tpu_custom_call" | custom-call | tf_op jit(solution)/shard_map/pallas_call | solution.py:241
  66.0 1.0 %copy.9 = bf16[1,128,4096]{2,1,0:T(8,128)(2,1)} copy(bf16[1,128,4096]{2,1,0:T(8,128)(2,1)S(1)} %bitcast.3) | data formatting | bytes 2097152
  66.9 0.6 copy.10
Async XLA Ops:
  0.6 0.9 %copy-start.1 = (f32[1,256]{1,0:T(1,128)S(1)}, f32[1,256]{1,0:T(1,128)}, u32[]{:S(2)}) copy-start(f32[1,256]{1,0:T(1,128)} %piv_ref.1) | copy-start | bytes 3076
  0.6 0.9 %copy-start.2 = (s32[1,16]{1,0:T(1,128)S(1)}, s32[1,16]{1,0:T(1,128)}, u32[]{:S(2)}) copy-start(s32[1,16]{1,0:T(1,128)} %pat_ref.1) | copy-start | bytes 196
  1.5 1.2 %copy-start = (bf16[1,128,4096]{2,1,0:T(8,128)(2,1)S(1)}, bf16[1,128,4096]{2,1,0:T(8,128)(2,1)}, u32[]{:S(2)}) copy-start(bf16[1,128,4096]{2,1,0:T(8,128)(2,1)} %param.5) | copy-start | bytes 3145732

commit v3 on v2

v3 whole, which is shorter than its diff:
```python
import jax
import jax.numpy as jnp
from jax import lax
from jax.experimental import pallas as pl
from jax.experimental.pallas import tpu as pltpu
from jax.sharding import PartitionSpec as P

MESH = pl.DeviceIdType.MESH
F32, BF16 = jnp.float32, jnp.bfloat16
NX, NY, NC, NZ = 2, 4, 2, 16
ROWS, SEG = 128, 256
CHUNKS = 4
DEEP = 1024
FAR = 4


def kernel(
    a_ref, f_ref, pat_ref, piv_ref, out_ref, var_ref,
    raw, masked, anc, packed, cov, vpart, vgot,
    hello, a_sem, s_send, s_recv, l_sem, y_send, y_recv, w_send, w_recv,
    z_send, z_recv, x_send, x_recv, o_send, o_recv, o_local, v_send, v_recv,
):
    leaf, grid = lax.axis_index("leaf"), lax.axis_index("grid")
    xh, z = leaf // NZ, lax.rem(leaf, NZ)
    x, y, c = grid // (NY * NC), lax.rem(grid // NC, NY), lax.rem(grid, NC)
    place_x = xh * NX + x

    def up_y(dy):
        return lax.rem(y + dy, NY)

    def up_z(dz):
        return lax.rem(z + dz + NZ, NZ)

    def other(v, d):
        return lax.rem(v + d, 2)

    def group(dx, dy, dc):
        return (leaf, other(x, dx) * NY * NC + up_y(dy) * NC + other(c, dc))

    def along_z(dz):
        return (xh * NZ + up_z(dz), grid)

    def chip_x(d):
        at = lax.rem(place_x + d, 2 * NX)
        return at // NX, lax.rem(at, NX)

    def along_x(d):
        h, low = chip_x(d)
        return (h * NZ + z, low * NY * NC + y * NC + c)

    core_mate = group(0, 0, 1)
    square = [(0, 1), (1, 0), (1, 1)]
    steps_z = [s * d for d in range(1, FAR + 1) for s in (1, -1)]
    sends = []

    def remote(src, dst, send, recv, to):
        return pltpu.make_async_remote_copy(
            src_ref=src, dst_ref=dst, send_sem=send, recv_sem=recv, device_id=to, device_id_type=MESH
        )

    def send(*copy):
        handle = remote(*copy)
        handle.start()
        sends.append(handle)

    def wait(ref, sem):
        remote(ref, ref, a_sem, sem, core_mate).wait_recv()

    def columns(side, t, cc):
        return pl.ds(pl.multiple_of(((side * NY + t) * NC + cc) * SEG, SEG), SEG)

    a_copy = pltpu.make_async_copy(a_ref, packed.at[z], a_sem)
    a_copy.start()
    known = [group(dx, 0, dc) for dx, dc in square] + [group(0, dy, 0) for dy in (1, 2, 3)]
    outer = lax.rem(place_x + jnp.where(x == 0, 3, 1), 2 * NX)
    outer_id = ((outer // NX) * NZ + z, lax.rem(outer, NX) * NY * NC + y * NC + c)
    known.append(outer_id)
    barrier = pltpu.get_barrier_semaphore()
    for to in known:
        pl.semaphore_signal(barrier, inc=1, device_id=to, device_id_type=MESH)
    lower = jnp.int32(0)
    for d in steps_z:
        lower += (up_z(d) < z).astype(jnp.int32)

        @pl.when(up_z(d) > z)
        def _(d=d):
            pl.semaphore_signal(barrier, inc=1, device_id=along_z(d), device_id_type=MESH)

    pl.semaphore_wait(barrier, len(known) + lower)
    for d in steps_z:

        @pl.when(up_z(d) < z)
        def _(d=d):
            pl.semaphore_signal(hello, inc=1, device_id=along_z(d), device_id_type=MESH)

    def way(d):
        return (0, d - 1) if d > 0 else (1, -d - 1)

    def send_z(origin, d):
        to = way(d - origin)
        send(packed.at[up_z(origin)], packed.at[up_z(origin)], z_send.at[*to], z_recv.at[*to], along_z(d))

    def wait_z(d):
        wait(packed.at[up_z(-d)], z_recv.at[*way(d)])

    def swap(t):
        mine = raw.at[t, x, y, c]
        for k, (dx, dc) in enumerate(square):
            part = f_ref.at[:, columns(other(x, dx), t, other(c, dc))]
            send(part, mine, s_send.at[t, k], s_recv.at[t, k], group(dx, 0, dc))
        here = f_ref.at[:, columns(x, t, c)]
        up_and_down(t, here, x, c)
        local = pltpu.make_async_copy(here, mine, l_sem.at[t])
        local.start()
        return local

    def up_and_down(t, src, side, cc):
        for k, dy in enumerate((1, 3)):
            send(src, raw.at[t, side, y, cc], y_send.at[t, k, side, cc], y_recv.at[t, k, side, cc], group(0, dy, 0))

    def spread(t):
        for k, (dx, dc) in enumerate(square):
            side, cc = other(x, dx), other(c, dc)
            part = raw.at[t, side, y, cc]
            wait(part, s_recv.at[t, k])
            up_and_down(t, part, side, cc)

    def hand_on(t):
        for dc in range(NC):
            cc = other(c, dc)
            for dx in range(NX):
                for k, dy in enumerate((1, 3)):
                    side = other(x, dx)
                    part = raw.at[t, side, up_y(NY - dy), cc]
                    wait(part, y_recv.at[t, k, side, cc])

                    @pl.when(side == k)
                    def _(k=k, dy=dy, part=part, cc=cc):
                        remote(part, part, w_send.at[t, k, cc], w_recv.at[t, k, cc], group(0, dy, 0)).start()

    def complete(t):
        for k in range(2):
            for cc in range(NC):
                wait(raw.at[t, k, up_y(2), cc], w_recv.at[t, k, cc])
        locals_[t].wait()

    locals_ = [swap(0), swap(1)]
    spread(0)

    higher = jnp.int32(0)
    for d in steps_z:
        higher += (up_z(d) > z).astype(jnp.int32)
    a_copy.wait()

    @pl.when(higher > 0)
    def _():
        pl.semaphore_wait(hello, higher)

    for d in reversed(steps_z):
        send_z(0, d)
    locals_.append(swap(2))
    spread(1)
    locals_.append(swap(3))

    wait_z(FAR)
    for d in range(FAR, 0, -1):
        send_z(-FAR, d)
    wait_z(-FAR)
    for d in range(1 - FAR, 0):
        send_z(FAR, d)
    spread(2)
    spread(3)

    for d in range(1, NZ // 2 + 1):
        for s in (1, -1):
            if d != FAR and s * d != -NZ // 2:
                wait_z(s * d)
    for k in range(NZ // 2):
        anc[xh, x, c, :, k * 128 : k * 128 + 128] = packed[2 * k : 2 * k + 2].reshape(128, ROWS).T

    mine = anc.at[xh, x, c]
    for k, d in enumerate((1, 3)):
        send(mine, mine, x_send.at[k], x_recv.at[k], along_x(d))
    send(mine, mine, x_send.at[2], x_recv.at[2], core_mate)

    hand_on(0)
    hand_on(1)

    for k, d in enumerate((1, 3)):
        h, low = chip_x(2 * NX - d)
        part = anc.at[h, low, c]
        wait(part, x_recv.at[k])
        some = part.at[k * 64 : k * 64 + 64]
        send(some, some, x_send.at[3 + k], x_recv.at[3 + k], along_x(d))
        send(part, part, x_send.at[5 + k], x_recv.at[5 + k], core_mate)
    hand_on(2)
    hand_on(3)

    def keep(t):
        complete(t)

        def keep_block(g, _):
            one = jnp.full((ROWS, SEG), pat_ref[0, g].astype(F32), F32).astype(BF16)
            side, yy, cc = g // (NY * NC), lax.rem(g // NC, NY), lax.rem(g, NC)
            masked[t, side, yy, cc] = raw[t, side, yy, cc] * one
            return 0

        lax.fori_loop(0, NX * NY * NC, keep_block, 0)

    def product(t, k, dx, dc):
        side, cc = other(x, dx), other(c, dc)
        total = jnp.zeros((ROWS, SEG), F32)
        for h in range(2):
            total += jnp.dot(anc[h, side, cc], masked[t, h].reshape(DEEP, SEG), preferred_element_type=F32)
        cross = -total
        terms = masked[t, side, y, cc].astype(F32) * cross
        vpart[t] += jnp.sum(terms.reshape(ROWS // 8, 8, SEG), axis=0)
        cov[t, side, cc] = cross.astype(BF16)
        there, part = out_ref.at[:, columns(x, t, c)], cov.at[t, side, cc]
        if k is None:
            pltpu.make_async_copy(part, there, o_local.at[t]).start()
        else:
            send(part, there, o_send.at[t, k], o_recv.at[t, k], group(dx, 0, dc))

    def far_rows(t):
        keep(t)
        product(t, 1, 1, 0)
        if t == 0:
            for k, d in enumerate((1, 3)):
                hh, ll = chip_x(2 * NX - d)
                wait(anc.at[hh, ll, other(c, 1)], x_recv.at[5 + k])
        product(t, 2, 1, 1)

    def near_rows(t):
        if t == 0:
            hh, ll = chip_x(2)
            for k in range(2):
                some = anc.at[hh, ll, c, k * 64 : k * 64 + 64]
                wait(some, x_recv.at[3 + k])
                send(some, some, x_send.at[7 + k], x_recv.at[7 + k], core_mate)
            product(t, None, 0, 0)
            wait(anc.at[xh, x, other(c, 1)], x_recv.at[2])
            for k in range(2):
                wait(anc.at[hh, ll, other(c, 1), k * 64 : k * 64 + 64], x_recv.at[7 + k])
            product(t, 0, 0, 1)
        else:
            product(t, 0, 0, 1)
            product(t, None, 0, 0)

    vpart[...] = jnp.zeros_like(vpart)
    far_rows(0)
    far_rows(1)
    near_rows(0)
    far_rows(2)
    near_rows(1)
    far_rows(3)
    near_rows(2)
    near_rows(3)

    for k, dy in enumerate((1, 2, 3)):
        send(vpart.at[up_y(dy)], vgot.at[k], v_send.at[k], v_recv.at[k], group(0, dy, 0))
    for t in range(CHUNKS):
        for k, (dx, dc) in enumerate(square):
            wait(out_ref.at[:, columns(other(x, dx), t, other(c, dc))], o_recv.at[t, k])
        there = out_ref.at[:, columns(x, t, c)]
        pltpu.make_async_copy(cov.at[t, x, c], there, o_local.at[t]).wait()
    total = vpart[y]
    for k in range(3):
        wait(vgot.at[k], v_recv.at[k])
        total += vgot[k]
    var_ref[...] = piv_ref[...] - jnp.sum(total, axis=0, keepdims=True)
    for handle in sends:
        handle.wait_send()
    for t in range(CHUNKS):
        for k in range(2):
            for cc in range(NC):
                part = raw.at[t, k, y, cc]
                remote(part, part, w_send.at[t, k, cc], w_recv.at[t, k, cc], core_mate).wait_send()


def on_device(ancestor_inverse, factor_block, block_pattern, pivot_inverse):
    rows, wide = factor_block.shape[1:]
    dma = pltpu.SemaphoreType.DMA
    vmem, hbm = pl.BlockSpec(memory_space=pltpu.VMEM), pl.BlockSpec(memory_space=pltpu.HBM)
    cross_cov, variances = pl.pallas_call(
        kernel,
        out_shape=(
            jax.ShapeDtypeStruct((rows, wide), BF16),
            jax.ShapeDtypeStruct(pivot_inverse.shape, F32),
        ),
        in_specs=[hbm, hbm, pl.BlockSpec(memory_space=pltpu.SMEM), vmem],
        out_specs=(hbm, vmem),
        scratch_shapes=[
            pltpu.VMEM((CHUNKS, NX, NY, NC, ROWS, SEG), BF16),
            pltpu.VMEM((CHUNKS, NX, NY, NC, ROWS, SEG), BF16),
            pltpu.VMEM((2, NX, NC, ROWS, DEEP), BF16),
            pltpu.VMEM((NZ, 64, ROWS), BF16),
            pltpu.VMEM((CHUNKS, NX, NC, ROWS, SEG), BF16),
            pltpu.VMEM((CHUNKS, 8, SEG), F32),
            pltpu.VMEM((3, 8, SEG), F32),
            pltpu.SemaphoreType.REGULAR, dma, dma((CHUNKS, 3)), dma((CHUNKS, 3)), dma((CHUNKS,)),
            dma((CHUNKS, 2, 2, 2)), dma((CHUNKS, 2, 2, 2)), dma((CHUNKS, 2, 2)), dma((CHUNKS, 2, 2)),
            dma((2, 8)), dma((2, 8)), dma((9,)), dma((9,)),
            dma((CHUNKS, 3)), dma((CHUNKS, 3)), dma((CHUNKS,)), dma((3,)), dma((3,)),
        ],
        compiler_params=pltpu.CompilerParams(
            collective_id=0, has_side_effects=True, vmem_limit_bytes=60 << 20
        ),
    )(ancestor_inverse.T, factor_block[0], block_pattern, pivot_inverse)
    return cross_cov[None], variances


def solution(mesh):
    return jax.shard_map(
        on_device,
        mesh=mesh,
        in_specs=(P("grid", "leaf"), P("leaf", "grid", None), P("leaf", None), P("leaf", "grid")),
        out_specs=(P("leaf", "grid", None), P("leaf", "grid")),
        check_vma=False,
    )
```

time: 67.7 us -> 60.4 us (0.89)
  Pallas kernels: 63.2 us -> 56.7 us
  local copies, waits for them, and re-layouts: 3.6 us -> 2.85 us
    pallas_call x1, Pallas kernels: 63.2 us -> 56.7 us  [on_device(): pl.pallas_call(kernel, out_shape=(jax.ShapeDtypeStruct((rows, wide), BF16...]
    unnamed x9 -> x4, local copies, waits for them, and re-layouts: 3.6 us -> 2.85 us
where the time goes in v3:
time: 60.4 us; the launch traced here: 60.2 us
  Pallas kernels  56.7 us (94%)
  local copies, waits for them, and re-layouts  2.85 us (5%)
  between operations  0.65 us (1%)
    pallas_call x1, Pallas kernels, on_device(): pl.pallas_call(kernel, out_shape=(jax.ShapeDtypeStruct((rows, wide), BF16...  56.7 us
    unnamed x4, local copies, waits for them, and re-layouts  2.85 us

profile of v3, /device:TPU:1, one launch (start us, length us, event | category | flops | bytes accessed | tf_op | source)
XLA Modules:
  0.0 60.2 jit_solution(2160635184133037340)
XLA Ops:
  0.6 56.7 %shard_map.59 = (bf16[128,4096]{1,0:T(8,128)(2,1)}, f32[1,256]{1,0:T(1,128)}) custom-call(bf16[64,128]{1,0:T(8,128)(2,1)} %bitcast.5, bf16[128,4096]{1,0:T(8,128)(2,1)} %bitcast.3, s32[1,16]{1,0:T(1,128)} %pat_ref.1, f32[1,256]{1,0:T(1,128)} %piv_ref.1), custom_call_target="tpu_custom_call" | custom-call | tf_op jit(solution)/shard_map/pallas_call | solution.py:285
  57.3 0.0 copy-start
  57.3 2.3 %copy.8 = bf16[1,128,4096]{2,1,0:T(8,128)(2,1)} copy(bf16[1,128,4096]{2,1,0:T(8,128)(2,1)} %bitcast.4) | data formatting | bytes 2097152
  59.6 0.0 copy-done
  59.6 0.6 copy.9
Async XLA Ops:
  57.3 2.3 %copy-start = (f32[1,256]{1,0:T(1,128)S(1)}, f32[1,256]{1,0:T(1,128)}, u32[]{:S(2)}) copy-start(f32[1,256]{1,0:T(1,128)} %get-tuple-element.9) | copy-start | bytes 3076

commit v4 on v3

v4 whole, which is shorter than its diff:
```python
import jax
import jax.numpy as jnp
from jax import lax
from jax.experimental import pallas as pl
from jax.experimental.pallas import tpu as pltpu
from jax.sharding import PartitionSpec as P

MESH = pl.DeviceIdType.MESH
F32, BF16 = jnp.float32, jnp.bfloat16
NX, NY, NC, NZ = 2, 4, 2, 16
ROWS, SEG = 128, 256
CHUNKS = 4
DEEP = 1024
FAR = 4


def kernel(
    a_ref, f_ref, pat_in, piv_in, out_ref, var_ref,
    raw, masked, anc, packed, cov, vpart, vgot, pat_ref, piv_ref,
    hello, a_sem, p_sem, s_send, s_recv, l_sem, y_send, y_recv, w_send, w_recv,
    z_send, z_recv, x_send, x_recv, o_send, o_recv, o_local, v_send, v_recv,
):
    leaf, grid = lax.axis_index("leaf"), lax.axis_index("grid")
    xh, z = leaf // NZ, lax.rem(leaf, NZ)
    x, y, c = grid // (NY * NC), lax.rem(grid // NC, NY), lax.rem(grid, NC)
    place_x = xh * NX + x

    def up_y(dy):
        return lax.rem(y + dy, NY)

    def up_z(dz):
        return lax.rem(z + dz + NZ, NZ)

    def other(v, d):
        return lax.rem(v + d, 2)

    def group(dx, dy, dc):
        return (leaf, other(x, dx) * NY * NC + up_y(dy) * NC + other(c, dc))

    def along_z(dz):
        return (xh * NZ + up_z(dz), grid)

    def chip_x(d):
        at = lax.rem(place_x + d, 2 * NX)
        return at // NX, lax.rem(at, NX)

    def along_x(d):
        h, low = chip_x(d)
        return (h * NZ + z, low * NY * NC + y * NC + c)

    core_mate = group(0, 0, 1)
    square = [(0, 1), (1, 0), (1, 1)]
    steps_z = [s * d for d in range(1, FAR + 1) for s in (1, -1)]
    sends = []

    def remote(src, dst, send, recv, to):
        return pltpu.make_async_remote_copy(
            src_ref=src, dst_ref=dst, send_sem=send, recv_sem=recv, device_id=to, device_id_type=MESH
        )

    def send(*copy):
        handle = remote(*copy)
        handle.start()
        sends.append(handle)

    def wait(ref, sem):
        remote(ref, ref, a_sem, sem, core_mate).wait_recv()

    def columns(side, t, cc):
        return pl.ds(pl.multiple_of(((side * NY + t) * NC + cc) * SEG, SEG), SEG)

    a_copy = pltpu.make_async_copy(a_ref, packed.at[z], a_sem)
    a_copy.start()
    small = [
        pltpu.make_async_copy(pat_in, pat_ref, p_sem.at[0]),
        pltpu.make_async_copy(piv_in, piv_ref, p_sem.at[1]),
    ]
    for copy in small:
        copy.start()
    known = [group(dx, 0, dc) for dx, dc in square] + [group(0, dy, 0) for dy in (1, 2, 3)]
    outer = lax.rem(place_x + jnp.where(x == 0, 3, 1), 2 * NX)
    outer_id = ((outer // NX) * NZ + z, lax.rem(outer, NX) * NY * NC + y * NC + c)
    known.append(outer_id)
    barrier = pltpu.get_barrier_semaphore()
    for to in known:
        pl.semaphore_signal(barrier, inc=1, device_id=to, device_id_type=MESH)
    late = z >= NZ // 2
    heard, answers = jnp.int32(0), jnp.int32(0)
    for d in steps_z:
        tells = (up_z(d) > z) | (late & (up_z(d) >= NZ // 2))
        heard += ((up_z(d) < z) | (late & (up_z(d) >= NZ // 2))).astype(jnp.int32)
        answers += ((up_z(d) > z) & jnp.logical_not(late)).astype(jnp.int32)

        @pl.when(tells)
        def _(d=d):
            pl.semaphore_signal(barrier, inc=1, device_id=along_z(d), device_id_type=MESH)

    pl.semaphore_wait(barrier, len(known) + heard)
    for d in steps_z:

        @pl.when((up_z(d) < z) & (up_z(d) < NZ // 2))
        def _(d=d):
            pl.semaphore_signal(hello, inc=1, device_id=along_z(d), device_id_type=MESH)

    def way(d):
        return (0, d - 1) if d > 0 else (1, -d - 1)

    def wait_z(d):
        wait(packed.at[up_z(-d)], z_recv.at[*way(d)])

    def each(low, high, body):
        def step(t, _):
            body(t)
            return 0

        lax.fori_loop(low, high, step, 0)

    def own_copy(t):
        return pltpu.make_async_copy(f_ref.at[:, columns(x, t, c)], raw.at[t, x, y, c], l_sem.at[t])

    def swap_copies(t):
        mine = raw.at[t, x, y, c]
        return [
            remote(
                f_ref.at[:, columns(other(x, dx), t, other(c, dc))],
                mine, s_send.at[t, k], s_recv.at[t, k], group(dx, 0, dc),
            )
            for k, (dx, dc) in enumerate(square)
        ]

    def y_copies(t, src, dx, dc):
        side, cc = other(x, dx), other(c, dc)
        return [
            remote(
                src, raw.at[t, side, y, cc],
                y_send.at[t, k, side, cc], y_recv.at[t, k, side, cc], group(0, dy, 0),
            )
            for k, dy in enumerate((1, 3))
        ]

    def swap(t):
        for copy in y_copies(t, f_ref.at[:, columns(x, t, c)], 0, 0) + swap_copies(t) + [own_copy(t)]:
            copy.start()

    def spread(t):
        for k, (dx, dc) in enumerate(square):
            part = raw.at[t, other(x, dx), y, other(c, dc)]
            wait(part, s_recv.at[t, k])
            for copy in y_copies(t, part, dx, dc):
                copy.start()

    def hand_copy(t, k, cc, at):
        part = raw.at[t, k, at, cc]
        return remote(part, part, w_send.at[t, k, cc], w_recv.at[t, k, cc], group(0, (1, 3)[k], 0))

    def hand_on(t):
        for dc in range(NC):
            cc = other(c, dc)
            for side in range(NX):
                for k in (side, 1 - side):
                    at = up_y(NY - (1, 3)[k])
                    wait(raw.at[t, side, at, cc], y_recv.at[t, k, side, cc])
                    if side == k:
                        hand_copy(t, k, cc, at).start()

    def complete(t):
        for k in range(2):
            for cc in range(NC):
                wait(raw.at[t, k, up_y(2), cc], w_recv.at[t, k, cc])
        own_copy(t).wait()

    def start_z():
        a_copy.wait()
        for d in reversed(steps_z):
            part = packed.at[z]
            remote(part, part, z_send.at[*way(d)], z_recv.at[*way(d)], along_z(d)).start()

    each(0, CHUNKS, swap)

    @pl.when(late)
    def _():
        start_z()

    spread(0)

    @pl.when(jnp.logical_not(late))
    def _():
        pl.semaphore_wait(hello, answers)
        start_z()

    def second_z():
        for far, ds in ((FAR, range(FAR, 0, -1)), (-FAR, range(1 - FAR, 0))):
            wait_z(far)
            for d in ds:
                part, to = packed.at[up_z(-far)], way(d + far)
                remote(part, part, z_send.at[*to], z_recv.at[*to], along_z(d)).start()

    spread(1)
    second_z()
    each(2, CHUNKS, spread)

    for d in range(1, NZ // 2 + 1):
        for s in (1, -1):
            if d != FAR and s * d != -NZ // 2:
                wait_z(s * d)
    for k in range(NZ // 2):
        anc[xh, x, c, :, k * 128 : k * 128 + 128] = packed[2 * k : 2 * k + 2].reshape(128, ROWS).T

    def rows(h, low, cc, half):
        return anc.at[h, low, cc, half * 64 : half * 64 + 64]

    for first in range(2):
        for k, d in enumerate((1, 3)):
            half = (k + first) % 2
            part = rows(xh, x, c, half)
            send(part, part, x_send.at[k, half], x_recv.at[k, half], along_x(d))
    send(anc.at[xh, x, c], anc.at[xh, x, c], x_send.at[2, 0], x_recv.at[2, 0], core_mate)

    each(0, 2, hand_on)

    for first in range(2):
        for k, d in enumerate((1, 3)):
            half = (k + first) % 2
            part = rows(*chip_x(2 * NX - d), c, half)
            wait(part, x_recv.at[k, half])
            if first == 0:
                send(part, part, x_send.at[3, k], x_recv.at[3, k], along_x(d))
            send(part, part, x_send.at[4 + k, half], x_recv.at[4 + k, half], core_mate)
    each(2, CHUNKS, hand_on)

    def keep(t):
        complete(t)

        def keep_block(g):
            one = jnp.full((ROWS, SEG), pat_ref[0, g].astype(F32), F32).astype(BF16)
            side, yy, cc = g // (NY * NC), lax.rem(g // NC, NY), lax.rem(g, NC)
            masked[t, side, yy, cc] = raw[t, side, yy, cc] * one

        each(0, NX * NY * NC, keep_block)

    def result_copy(t, k):
        dx, dc = square[k]
        part, there = cov.at[t, other(x, dx), other(c, dc)], out_ref.at[:, columns(x, t, c)]
        return remote(part, there, o_send.at[t, k], o_recv.at[t, k], group(dx, 0, dc))

    def own_result(t):
        return pltpu.make_async_copy(cov.at[t, x, c], out_ref.at[:, columns(x, t, c)], o_local.at[t])

    def near_ready():
        for k in range(2):
            part = rows(*chip_x(2), c, k)
            wait(part, x_recv.at[3, k])
            remote(part, part, x_send.at[6, k], x_recv.at[6, k], core_mate).start()
        wait(anc.at[xh, x, other(c, 1)], x_recv.at[2, 0])
        for k in range(2):
            wait(rows(*chip_x(2), other(c, 1), k), x_recv.at[6, k])

    def product(i):
        far = (i < 2) | ((lax.rem(i, 2) == 1) & (i < 7))
        t = (i + 1) // 2 - jnp.where(far, 0, 1)
        side = jnp.where(far, 1 - x, x)

        @pl.when(far)
        def _():
            keep(t)

        @pl.when(i == 2)
        def _():
            near_ready()

        total = jnp.zeros((NC * ROWS, SEG), F32)
        for h in range(2):
            total += jnp.dot(
                anc[h, side].reshape(NC * ROWS, DEEP), masked[t, h].reshape(DEEP, SEG), preferred_element_type=F32
            )
        cross = -total
        terms = masked[t, side, y].reshape(NC * ROWS, SEG).astype(F32) * cross
        vpart[t] += jnp.sum(terms.reshape(NC * ROWS // 8, 8, SEG), axis=0)
        cov[t, side] = cross.astype(BF16).reshape(NC, ROWS, SEG)

        @pl.when(far)
        def _():
            result_copy(t, 1).start()
            result_copy(t, 2).start()

        @pl.when(jnp.logical_not(far))
        def _():
            result_copy(t, 0).start()
            own_result(t).start()

    vpart[...] = jnp.zeros_like(vpart)
    for copy in small:
        copy.wait()
    for k, d in enumerate((1, 3)):
        for half in range(2):
            wait(rows(*chip_x(2 * NX - d), other(c, 1), half), x_recv.at[4 + k, half])
    each(0, 2 * CHUNKS, product)

    for k, dy in enumerate((1, 2, 3)):
        send(vpart.at[up_y(dy)], vgot.at[k], v_send.at[k], v_recv.at[k], group(0, dy, 0))

    def results(t):
        for k, (dx, dc) in enumerate(square):
            wait(out_ref.at[:, columns(other(x, dx), t, other(c, dc))], o_recv.at[t, k])
        own_result(t).wait()

    each(0, CHUNKS, results)
    total = vpart[y]
    for k in range(3):
        wait(vgot.at[k], v_recv.at[k])
        total += vgot[k]
    var_ref[...] = piv_ref[...] - jnp.sum(total, axis=0, keepdims=True)
    for handle in sends:
        handle.wait_send()
    for k in range(2):
        remote(rows(xh, x, c, k), rows(xh, x, c, k), x_send.at[6, k], x_recv.at[6, k], core_mate).wait_send()
    for d in range(1 - NZ // 2, NZ // 2 + 1):
        if d:
            remote(packed.at[z], packed.at[z], z_send.at[*way(d)], z_recv.at[*way(d)], core_mate).wait_send()

    def sent(t):
        for copy in swap_copies(t):
            copy.wait_send()
        for dx in range(NX):
            for dc in range(NC):
                for copy in y_copies(t, raw.at[t, x, y, c], dx, dc):
                    copy.wait_send()
        for k in range(2):
            for cc in range(NC):
                hand_copy(t, k, cc, y).wait_send()
        for k in range(3):
            result_copy(t, k).wait_send()

    each(0, CHUNKS, sent)


def hand_over(cross_ref, var_ref, cross_out, var_out, cross, var, sems):
    parts = [pl.ds(k * ROWS // 4, ROWS // 4) for k in range(4)]
    through = [(cross_ref.at[p], cross.at[p], cross_out.at[0, p]) for p in parts] + [(var_ref, var, var_out)]
    loads = [pltpu.make_async_copy(a, b, sems.at[k]) for k, (a, b, _) in enumerate(through)]
    stores = [pltpu.make_async_copy(b, c, sems.at[5 + k]) for k, (_, b, c) in enumerate(through)]
    for load in loads:
        load.start()
    for load, store in zip(loads, stores):
        load.wait()
        store.start()
    for store in stores:
        store.wait()


def on_device(ancestor_inverse, factor_block, block_pattern, pivot_inverse):
    rows, wide = factor_block.shape[1:]
    dma = pltpu.SemaphoreType.DMA
    vmem, hbm = pl.BlockSpec(memory_space=pltpu.VMEM), pl.BlockSpec(memory_space=pltpu.HBM)
    cross_cov, variances = pl.pallas_call(
        kernel,
        out_shape=(
            jax.ShapeDtypeStruct((rows, wide), BF16),
            jax.ShapeDtypeStruct(pivot_inverse.shape, F32),
        ),
        in_specs=[hbm] * 4,
        out_specs=(hbm, vmem),
        scratch_shapes=[
            pltpu.VMEM((CHUNKS, NX, NY, NC, ROWS, SEG), BF16),
            pltpu.VMEM((CHUNKS, NX, NY, NC, ROWS, SEG), BF16),
            pltpu.VMEM((2, NX, NC, ROWS, DEEP), BF16),
            pltpu.VMEM((NZ, 64, ROWS), BF16),
            pltpu.VMEM((CHUNKS, NX, NC, ROWS, SEG), BF16),
            pltpu.VMEM((CHUNKS, 8, SEG), F32),
            pltpu.VMEM((3, 8, SEG), F32),
            pltpu.SMEM(block_pattern.shape, jnp.int32),
            pltpu.VMEM(pivot_inverse.shape, F32),
            pltpu.SemaphoreType.REGULAR, dma, dma((2,)), dma((CHUNKS, 3)), dma((CHUNKS, 3)), dma((CHUNKS,)),
            dma((CHUNKS, 2, 2, 2)), dma((CHUNKS, 2, 2, 2)), dma((CHUNKS, 2, 2)), dma((CHUNKS, 2, 2)),
            dma((2, 8)), dma((2, 8)), dma((7, 2)), dma((7, 2)),
            dma((CHUNKS, 3)), dma((CHUNKS, 3)), dma((CHUNKS,)), dma((3,)), dma((3,)),
        ],
        compiler_params=pltpu.CompilerParams(
            collective_id=0, has_side_effects=True, vmem_limit_bytes=60 << 20
        ),
    )(ancestor_inverse.T, factor_block[0], block_pattern, pivot_inverse)
    return pl.pallas_call(
        hand_over,
        out_shape=(
            jax.ShapeDtypeStruct((1, rows, wide), BF16),
            jax.ShapeDtypeStruct(pivot_inverse.shape, F32),
        ),
        in_specs=[hbm, hbm],
        out_specs=(hbm, hbm),
        scratch_shapes=[pltpu.VMEM((rows, wide), BF16), pltpu.VMEM(pivot_inverse.shape, F32), dma((10,))],
        compiler_params=pltpu.CompilerParams(vmem_limit_bytes=60 << 20),
    )(cross_cov, variances)


def solution(mesh):
    return jax.shard_map(
        on_device,
        mesh=mesh,
        in_specs=(P("grid", "leaf"), P("leaf", "grid", None), P("leaf", None), P("leaf", "grid")),
        out_specs=(P("leaf", "grid", None), P("leaf", "grid")),
        check_vma=False,
    )
```

time: 60.4 us -> 56.5 us (0.935)
  local copies, waits for them, and re-layouts: 2.85 us -> 0 us
  Pallas kernels: 56.7 us -> 55.8 us
    pallas_call x1, Pallas kernels: 56.7 us -> 53.8 us  [on_device(): pl.pallas_call(kernel, out_shape=(jax.ShapeDtypeStruct((rows, wide), BF16...]
    unnamed x4 -> x0, local copies, waits for them, and re-layouts: 2.85 us -> none
    pallas_call x0 -> x1, Pallas kernels: none -> 2 us  [on_device(): pl.pallas_call(hand_over, out_shape=(jax.ShapeDtypeStruct((1, rows, wide)...]
where the time goes in v4:
time: 56.5 us; the launch traced here: 56.4 us
  Pallas kernels  55.8 us (99%)
  between operations  0.64 us (1%)
    pallas_call x1, Pallas kernels, on_device(): pl.pallas_call(kernel, out_shape=(jax.ShapeDtypeStruct((rows, wide), BF16...  53.8 us
    pallas_call x1, Pallas kernels, on_device(): pl.pallas_call(hand_over, out_shape=(jax.ShapeDtypeStruct((1, rows, wide)...  2 us

profile of v4, /device:TPU:1, one launch (start us, length us, event | category | flops | bytes accessed | tf_op | source)
XLA Modules:
  0.0 56.4 jit_solution(15659259104000021595)
XLA Ops:
  0.6 53.8 %shard_map.59 = (bf16[128,4096]{1,0:T(8,128)(2,1)}, f32[1,256]{1,0:T(1,128)}) custom-call(bf16[64,128]{1,0:T(8,128)(2,1)} %bitcast.3, bf16[128,4096]{1,0:T(8,128)(2,1)} %bitcast.2, s32[1,16]{1,0:T(1,128)} %pat_in.1, f32[1,256]{1,0:T(1,128)} %piv_in.1), custom_call_target="tpu_custom_call" | custom-call | tf_op jit(solution)/shard_map/pallas_call | solution.py:355
  54.4 2.0 %shard_map.60 = (bf16[1,128,4096]{2,1,0:T(8,128)(2,1)}, f32[1,256]{1,0:T(1,128)}) custom-call(bf16[128,4096]{1,0:T(8,128)(2,1)} %get-tuple-element.4.cross_ref, f32[1,256]{1,0:T(1,128)} %get-tuple-element.5.var_ref), custom_call_target="tpu_custom_call" | custom-call | tf_op jit(solution)/shard_map/pallas_call | solution.py:382

commit v5 on v4

--- a/solution.py
+++ b/solution.py
@@ -17,7 +17,7 @@
 def kernel(
     a_ref, f_ref, pat_in, piv_in, out_ref, var_ref,
     raw, masked, anc, packed, cov, vpart, vgot, pat_ref, piv_ref,
-    hello, a_sem, p_sem, s_send, s_recv, l_sem, y_send, y_recv, w_send, w_recv,
+    hello, hello0, a_sem, p_sem, s_send, s_recv, l_sem, y_send, y_recv, w_send, w_recv,
     z_send, z_recv, x_send, x_recv, o_send, o_recv, o_local, v_send, v_recv,
 ):
     leaf, grid = lax.axis_index("leaf"), lax.axis_index("grid")
@@ -82,25 +82,61 @@
     outer_id = ((outer // NX) * NZ + z, lax.rem(outer, NX) * NY * NC + y * NC + c)
     known.append(outer_id)
     barrier = pltpu.get_barrier_semaphore()
-    for to in known:
-        pl.semaphore_signal(barrier, inc=1, device_id=to, device_id_type=MESH)
+    first = (leaf == 0) & (grid == 0)
+    square0 = (leaf == 0) & ((grid == 1) | (grid == NY * NC) | (grid == NY * NC + 1))
+    row0 = (leaf == 0) & ((grid == NC) | (grid == 2 * NC) | (grid == 3 * NC))
+    outer0 = (leaf == NZ) & (grid == NY * NC)
+    column0 = (grid == 0) & (leaf >= 1) & (leaf <= FAR)
+
+    def is_first(to):
+        return (to[0] == 0) & (to[1] == 0)
+
     late = z >= NZ // 2
-    heard, answers = jnp.int32(0), jnp.int32(0)
+
+    def rank(v):
+        return jnp.where(v < NZ // 2, v, jnp.where(v < 3 * NZ // 4, v + NZ // 4, v - NZ // 4))
+
+    def meets(d):
+        return late & (up_z(d) // (NZ // 4) == z // (NZ // 4))
+
+    def above(d):
+        return (rank(up_z(d)) > rank(z)) & jnp.logical_not(meets(d))
+
+    def below(d):
+        return (rank(up_z(d)) < rank(z)) & jnp.logical_not(meets(d))
+
+    waits = len(known) - (square0 | row0 | outer0).astype(jnp.int32)
+    answers = jnp.int32(0)
+
+    @pl.when(jnp.logical_not(first))
+    def _():
+        for to in known:
+            pl.semaphore_signal(barrier, inc=1, device_id=to, device_id_type=MESH)
+
+    def odd_pair(d):
+        return (first & (d > 0)) | (column0 & (up_z(d) == 0))
+
     for d in steps_z:
-        tells = (up_z(d) > z) | (late & (up_z(d) >= NZ // 2))
-        heard += ((up_z(d) < z) | (late & (up_z(d) >= NZ // 2))).astype(jnp.int32)
-        answers += ((up_z(d) > z) & jnp.logical_not(late)).astype(jnp.int32)
+        tells = (odd_pair(d) & column0) | (jnp.logical_not(odd_pair(d)) & (above(d) | meets(d)))
+        hears = (odd_pair(d) & first) | (jnp.logical_not(odd_pair(d)) & (below(d) | meets(d)))
+        waits += hears.astype(jnp.int32)
+        answers += (above(d) & jnp.logical_not(odd_pair(d))).astype(jnp.int32)
 
         @pl.when(tells)
         def _(d=d):
             pl.semaphore_signal(barrier, inc=1, device_id=along_z(d), device_id_type=MESH)
 
-    pl.semaphore_wait(barrier, len(known) + heard)
+    pl.semaphore_wait(barrier, waits)
     for d in steps_z:
 
-        @pl.when((up_z(d) < z) & (up_z(d) < NZ // 2))
+        @pl.when(below(d) & jnp.logical_not(odd_pair(d)))
         def _(d=d):
             pl.semaphore_signal(hello, inc=1, device_id=along_z(d), device_id_type=MESH)
+
+    @pl.when(first)
+    def _():
+        for to in known + [along_z(d) for d in range(1, FAR + 1)]:
+            pl.semaphore_signal(hello0, inc=1, device_id=to, device_id_type=MESH)
 
     def way(d):
         return (0, d - 1) if d > 0 else (1, -d - 1)
@@ -138,16 +174,35 @@
             for k, dy in enumerate((1, 3))
         ]
 
-    def swap(t):
-        for copy in y_copies(t, f_ref.at[:, columns(x, t, c)], 0, 0) + swap_copies(t) + [own_copy(t)]:
-            copy.start()
-
-    def spread(t):
+    neighbours = [group(0, dy, 0) for dy in (1, 3)]
+    mates = [group(dx, 0, dc) for dx, dc in square]
+
+    def start(copies, targets, to_first):
+        for copy, to in zip(copies, targets):
+
+            @pl.when(is_first(to) == to_first)
+            def _(copy=copy):
+                copy.start()
+
+    def swap(t, to_first=False):
+        start(y_copies(t, f_ref.at[:, columns(x, t, c)], 0, 0), neighbours, to_first)
+        start(swap_copies(t), mates, to_first)
+        if not to_first:
+            own_copy(t).start()
+
+    def spread(t, from_first=False):
         for k, (dx, dc) in enumerate(square):
+
+            @pl.when(is_first(mates[k]) == from_first)
+            def _(k=k, dx=dx, dc=dc):
+                part = raw.at[t, other(x, dx), y, other(c, dc)]
+                wait(part, s_recv.at[t, k])
+                start(y_copies(t, part, dx, dc), neighbours, False)
+
+    def spread_to_first(t):
+        for dx, dc in square:
             part = raw.at[t, other(x, dx), y, other(c, dc)]
-            wait(part, s_recv.at[t, k])
-            for copy in y_copies(t, part, dx, dc):
-                copy.start()
+            start(y_copies(t, part, dx, dc), neighbours, True)
 
     def hand_copy(t, k, cc, at):
         part = raw.at[t, k, at, cc]
@@ -177,16 +232,12 @@
 
     each(0, CHUNKS, swap)
 
-    @pl.when(late)
-    def _():
-        start_z()
-
-    spread(0)
-
-    @pl.when(jnp.logical_not(late))
-    def _():
-        pl.semaphore_wait(hello, answers)
-        start_z()
+    def rest(t):
+        spread(t)
+
+        @pl.when(row0)
+        def _():
+            spread_to_first(t)
 
     def second_z():
         for far, ds in ((FAR, range(FAR, 0, -1)), (-FAR, range(1 - FAR, 0))):
@@ -195,9 +246,57 @@
                 part, to = packed.at[up_z(-far)], way(d + far)
                 remote(part, part, z_send.at[*to], z_recv.at[*to], along_z(d)).start()
 
-    spread(1)
-    second_z()
-    each(2, CHUNKS, spread)
+    @pl.when(late)
+    def _():
+        @pl.when(answers > 0)
+        def _():
+            pl.semaphore_wait(hello, answers)
+
+        start_z()
+
+    spread(0)
+
+    @pl.when(square0 | row0 | outer0 | column0)
+    def _():
+        pl.semaphore_wait(hello0, 1)
+        each(0, CHUNKS, lambda t: swap(t, True))
+
+        @pl.when(row0)
+        def _():
+            spread_to_first(0)
+
+    @pl.when(late)
+    def _():
+        second_z()
+
+    def hello_z():
+        pl.semaphore_wait(hello, answers)
+        start_z()
+
+    @pl.when((z >= FAR) & (z < NZ // 2))
+    def _():
+        hello_z()
+
+    rest(1)
+
+    @pl.when((z >= FAR) & (z < NZ // 2))
+    def _():
+        second_z()
+
+    @pl.when(z < FAR)
+    def _():
+        hello_z()
+
+    each(2, CHUNKS, rest)
+
+    @pl.when(z < FAR)
+    def _():
+        second_z()
+
+    @pl.when(square0)
+    def _():
+        each(0, CHUNKS, lambda t: spread(t, True))
+
 
     for d in range(1, NZ // 2 + 1):
         for s in (1, -1):
@@ -370,7 +469,7 @@
             pltpu.VMEM((3, 8, SEG), F32),
             pltpu.SMEM(block_pattern.shape, jnp.int32),
             pltpu.VMEM(pivot_inverse.shape, F32),
-            pltpu.SemaphoreType.REGULAR, dma, dma((2,)), dma((CHUNKS, 3)), dma((CHUNKS, 3)), dma((CHUNKS,)),
+            pltpu.SemaphoreType.REGULAR, pltpu.SemaphoreType.REGULAR, dma, dma((2,)), dma((CHUNKS, 3)), dma((CHUNKS, 3)), dma((CHUNKS,)),
             dma((CHUNKS, 2, 2, 2)), dma((CHUNKS, 2, 2, 2)), dma((CHUNKS, 2, 2)), dma((CHUNKS, 2, 2)),
             dma((2, 8)), dma((2, 8)), dma((7, 2)), dma((7, 2)),
             dma((CHUNKS, 3)), dma((CHUNKS, 3)), dma((CHUNKS,)), dma((3,)), dma((3,)),

time: 56.5 us -> 55.3 us (0.979)
  Pallas kernels: 55.8 us -> 54.5 us
    pallas_call x1, Pallas kernels: 53.8 us -> 52.5 us  [on_device(): pl.pallas_call(kernel, out_shape=(jax.ShapeDtypeStruct((rows, wide), BF16...]
where the time goes in v5:
time: 55.3 us; the launch traced here: 55.1 us
  Pallas kernels  54.5 us (99%)
  between operations  0.64 us (1%)
    pallas_call x1, Pallas kernels, on_device(): pl.pallas_call(kernel, out_shape=(jax.ShapeDtypeStruct((rows, wide), BF16...  52.5 us
    pallas_call x1, Pallas kernels, on_device(): pl.pallas_call(hand_over, out_shape=(jax.ShapeDtypeStruct((1, rows, wide)...  2 us

profile of v5, /device:TPU:1, one launch (start us, length us, event | category | flops | bytes accessed | tf_op | source)
XLA Modules:
  0.0 55.1 jit_solution(3138991090224652909)
XLA Ops:
  0.6 52.5 %shard_map.59 = (bf16[128,4096]{1,0:T(8,128)(2,1)}, f32[1,256]{1,0:T(1,128)}) custom-call(bf16[64,128]{1,0:T(8,128)(2,1)} %bitcast.3, bf16[128,4096]{1,0:T(8,128)(2,1)} %bitcast.2, s32[1,16]{1,0:T(1,128)} %pat_in.1, f32[1,256]{1,0:T(1,128)} %piv_in.1), custom_call_target="tpu_custom_call" | custom-call | tf_op jit(solution)/shard_map/pallas_call | solution.py:454
  53.1 2.0 %shard_map.60 = (bf16[1,128,4096]{2,1,0:T(8,128)(2,1)}, f32[1,256]{1,0:T(1,128)}) custom-call(bf16[128,4096]{1,0:T(8,128)(2,1)} %get-tuple-element.4.cross_ref, f32[1,256]{1,0:T(1,128)} %get-tuple-element.5.var_ref), custom_call_target="tpu_custom_call" | custom-call | tf_op jit(solution)/shard_map/pallas_call | solution.py:481

commit v6 on v5

--- a/solution.py
+++ b/solution.py
@@ -230,7 +230,6 @@
             part = packed.at[z]
             remote(part, part, z_send.at[*way(d)], z_recv.at[*way(d)], along_z(d)).start()
 
-    each(0, CHUNKS, swap)
 
     def rest(t):
         spread(t)
@@ -246,12 +245,17 @@
                 part, to = packed.at[up_z(-far)], way(d + far)
                 remote(part, part, z_send.at[*to], z_recv.at[*to], along_z(d)).start()
 
-    @pl.when(late)
-    def _():
-        @pl.when(answers > 0)
-        def _():
-            pl.semaphore_wait(hello, answers)
-
+    each(0, 1, swap)
+
+    @pl.when(late & (answers == 0))
+    def _():
+        start_z()
+
+    each(1, CHUNKS, swap)
+
+    @pl.when(late & (answers > 0))
+    def _():
+        pl.semaphore_wait(hello, answers)
         start_z()
 
     spread(0)
@@ -387,13 +391,36 @@
             result_copy(t, 0).start()
             own_result(t).start()
 
+    def far_ready():
+        for k, d in enumerate((1, 3)):
+            for half in range(2):
+                wait(rows(*chip_x(2 * NX - d), other(c, 1), half), x_recv.at[4 + k, half])
+
+    def core_rows(cc):
+        total = jnp.zeros((ROWS, SEG), F32)
+        for h in range(2):
+            total += jnp.dot(anc[h, 1 - x, cc], masked[0, h].reshape(DEEP, SEG), preferred_element_type=F32)
+        cross = -total
+        terms = masked[0, 1 - x, y, cc].astype(F32) * cross
+        vpart[0] += jnp.sum(terms.reshape(ROWS // 8, 8, SEG), axis=0)
+        cov[0, 1 - x, cc] = cross.astype(BF16)
+
+        @pl.when(cc == c)
+        def _():
+            result_copy(0, 1).start()
+
+        @pl.when(cc != c)
+        def _():
+            result_copy(0, 2).start()
+
     vpart[...] = jnp.zeros_like(vpart)
     for copy in small:
         copy.wait()
-    for k, d in enumerate((1, 3)):
-        for half in range(2):
-            wait(rows(*chip_x(2 * NX - d), other(c, 1), half), x_recv.at[4 + k, half])
-    each(0, 2 * CHUNKS, product)
+    keep(0)
+    core_rows(c)
+    far_ready()
+    core_rows(1 - c)
+    each(1, 2 * CHUNKS, product)
 
     for k, dy in enumerate((1, 2, 3)):
         send(vpart.at[up_y(dy)], vgot.at[k], v_send.at[k], v_recv.at[k], group(0, dy, 0))

time: 55.3 us -> 54.3 us (0.982)
  Pallas kernels: 54.5 us -> 53.5 us
    pallas_call x1, Pallas kernels: 52.5 us -> 51.5 us  [on_device(): pl.pallas_call(kernel, out_shape=(jax.ShapeDtypeStruct((rows, wide), BF16...]
where the time goes in v6:
time: 54.3 us; the launch traced here: 54.1 us
  Pallas kernels  53.5 us (99%)
  between operations  0.64 us (1%)
    pallas_call x1, Pallas kernels, on_device(): pl.pallas_call(kernel, out_shape=(jax.ShapeDtypeStruct((rows, wide), BF16...  51.5 us
    pallas_call x1, Pallas kernels, on_device(): pl.pallas_call(hand_over, out_shape=(jax.ShapeDtypeStruct((1, rows, wide)...  2 us

profile of v6, /device:TPU:1, one launch (start us, length us, event | category | flops | bytes accessed | tf_op | source)
XLA Modules:
  0.0 54.1 jit_solution(2134533263348776183)
XLA Ops:
  0.6 51.5 %shard_map.59 = (bf16[128,4096]{1,0:T(8,128)(2,1)}, f32[1,256]{1,0:T(1,128)}) custom-call(bf16[64,128]{1,0:T(8,128)(2,1)} %bitcast.3, bf16[128,4096]{1,0:T(8,128)(2,1)} %bitcast.2, s32[1,16]{1,0:T(1,128)} %pat_in.1, f32[1,256]{1,0:T(1,128)} %piv_in.1), custom_call_target="tpu_custom_call" | custom-call | tf_op jit(solution)/shard_map/pallas_call | solution.py:481
  52.1 2.0 %shard_map.60 = (bf16[1,128,4096]{2,1,0:T(8,128)(2,1)}, f32[1,256]{1,0:T(1,128)}) custom-call(bf16[128,4096]{1,0:T(8,128)(2,1)} %get-tuple-element.4.cross_ref, f32[1,256]{1,0:T(1,128)} %get-tuple-element.5.var_ref), custom_call_target="tpu_custom_call" | custom-call | tf_op jit(solution)/shard_map/pallas_call | solution.py:508

commit v7 on v6

--- a/solution.py
+++ b/solution.py
@@ -349,25 +349,31 @@
     def own_result(t):
         return pltpu.make_async_copy(cov.at[t, x, c], out_ref.at[:, columns(x, t, c)], o_local.at[t])
 
-    def near_ready():
+    def near_forward():
         for k in range(2):
             part = rows(*chip_x(2), c, k)
             wait(part, x_recv.at[3, k])
             remote(part, part, x_send.at[6, k], x_recv.at[6, k], core_mate).start()
+
+    def near_ready():
         wait(anc.at[xh, x, other(c, 1)], x_recv.at[2, 0])
         for k in range(2):
             wait(rows(*chip_x(2), other(c, 1), k), x_recv.at[6, k])
 
     def product(i):
-        far = (i < 2) | ((lax.rem(i, 2) == 1) & (i < 7))
-        t = (i + 1) // 2 - jnp.where(far, 0, 1)
+        far = (i < 3) | (i == 5)
+        t = jnp.where(i < 3, i, jnp.where(i < 5, i - 3, jnp.where(i == 5, 3, i - 4)))
         side = jnp.where(far, 1 - x, x)
 
+        @pl.when(i == 2)
+        def _():
+            near_forward()
+
         @pl.when(far)
         def _():
             keep(t)
 
-        @pl.when(i == 2)
+        @pl.when(i == 3)
         def _():
             near_ready()
 

time: 54.3 us -> 54.3 us (level)
  no operation moved by 1% of the time
where the time goes in v7:
time: 54.3 us; the launch traced here: 54.1 us
  Pallas kernels  53.5 us (99%)
  between operations  0.64 us (1%)
    pallas_call x1, Pallas kernels, on_device(): pl.pallas_call(kernel, out_shape=(jax.ShapeDtypeStruct((rows, wide), BF16...  51.5 us
    pallas_call x1, Pallas kernels, on_device(): pl.pallas_call(hand_over, out_shape=(jax.ShapeDtypeStruct((1, rows, wide)...  2 us

profile of v7, /device:TPU:1, one launch (start us, length us, event | category | flops | bytes accessed | tf_op | source)
XLA Modules:
  0.0 54.1 jit_solution(2279832105871922687)
XLA Ops:
  0.6 51.5 %shard_map.59 = (bf16[128,4096]{1,0:T(8,128)(2,1)}, f32[1,256]{1,0:T(1,128)}) custom-call(bf16[64,128]{1,0:T(8,128)(2,1)} %bitcast.3, bf16[128,4096]{1,0:T(8,128)(2,1)} %bitcast.2, s32[1,16]{1,0:T(1,128)} %pat_in.1, f32[1,256]{1,0:T(1,128)} %piv_in.1), custom_call_target="tpu_custom_call" | custom-call | tf_op jit(solution)/shard_map/pallas_call | solution.py:487
  52.1 2.0 %shard_map.60 = (bf16[1,128,4096]{2,1,0:T(8,128)(2,1)}, f32[1,256]{1,0:T(1,128)}) custom-call(bf16[128,4096]{1,0:T(8,128)(2,1)} %get-tuple-element.4.cross_ref, f32[1,256]{1,0:T(1,128)} %get-tuple-element.5.var_ref), custom_call_target="tpu_custom_call" | custom-call | tf_op jit(solution)/shard_map/pallas_call | solution.py:514

commit v8 on v7

--- a/solution.py
+++ b/solution.py
@@ -467,10 +467,10 @@
 
 
 def hand_over(cross_ref, var_ref, cross_out, var_out, cross, var, sems):
-    parts = [pl.ds(k * ROWS // 4, ROWS // 4) for k in range(4)]
+    parts = [pl.ds(k * ROWS // 8, ROWS // 8) for k in range(8)]
     through = [(cross_ref.at[p], cross.at[p], cross_out.at[0, p]) for p in parts] + [(var_ref, var, var_out)]
     loads = [pltpu.make_async_copy(a, b, sems.at[k]) for k, (a, b, _) in enumerate(through)]
-    stores = [pltpu.make_async_copy(b, c, sems.at[5 + k]) for k, (_, b, c) in enumerate(through)]
+    stores = [pltpu.make_async_copy(b, c, sems.at[9 + k]) for k, (_, b, c) in enumerate(through)]
     for load in loads:
         load.start()
     for load, store in zip(loads, stores):
@@ -519,7 +519,7 @@
         ),
         in_specs=[hbm, hbm],
         out_specs=(hbm, hbm),
-        scratch_shapes=[pltpu.VMEM((rows, wide), BF16), pltpu.VMEM(pivot_inverse.shape, F32), dma((10,))],
+        scratch_shapes=[pltpu.VMEM((rows, wide), BF16), pltpu.VMEM(pivot_inverse.shape, F32), dma((18,))],
         compiler_params=pltpu.CompilerParams(vmem_limit_bytes=60 << 20),
     )(cross_cov, variances)
 

time: 54.3 us -> 54.4 us (level)
  no operation moved by 1% of the time
where the time goes in v8:
time: 54.4 us; the launch traced here: 54.2 us
  Pallas kernels  53.6 us (99%)
  between operations  0.64 us (1%)
    pallas_call x1, Pallas kernels, on_device(): pl.pallas_call(kernel, out_shape=(jax.ShapeDtypeStruct((rows, wide), BF16...  51.5 us
    pallas_call x1, Pallas kernels, on_device(): pl.pallas_call(hand_over, out_shape=(jax.ShapeDtypeStruct((1, rows, wide)...  2.11 us

profile of v8, /device:TPU:1, one launch (start us, length us, event | category | flops | bytes accessed | tf_op | source)
XLA Modules:
  0.0 54.2 jit_solution(12271311791416131449)
XLA Ops:
  0.6 51.5 %shard_map.59 = (bf16[128,4096]{1,0:T(8,128)(2,1)}, f32[1,256]{1,0:T(1,128)}) custom-call(bf16[64,128]{1,0:T(8,128)(2,1)} %bitcast.3, bf16[128,4096]{1,0:T(8,128)(2,1)} %bitcast.2, s32[1,16]{1,0:T(1,128)} %pat_in.1, f32[1,256]{1,0:T(1,128)} %piv_in.1), custom_call_target="tpu_custom_call" | custom-call | tf_op jit(solution)/shard_map/pallas_call | solution.py:487
  52.1 2.1 %shard_map.60 = (bf16[1,128,4096]{2,1,0:T(8,128)(2,1)}, f32[1,256]{1,0:T(1,128)}) custom-call(bf16[128,4096]{1,0:T(8,128)(2,1)} %get-tuple-element.4.cross_ref, f32[1,256]{1,0:T(1,128)} %get-tuple-element.5.var_ref), custom_call_target="tpu_custom_call" | custom-call | tf_op jit(solution)/shard_map/pallas_call | solution.py:514
